TPU v7x, 128 devices: a whole 4x4x4 slice. The times are simulated.
128 devices in a mesh: gx: 8 (over z_hi, x), gy: 16 (over z_lo, y, core).
Axes of the slice: x: 4, y: 4, z: 4 (z_hi: 2, z_lo: 2; z = z_hi * 2 + z_lo), core: 2. Of those that a mesh axis runs over, the one named last changes fastest.
Arguments:
- tracers: float32 [2, 8, 1024, 2048], P(None, None, 'gy', 'gx'), may hold values from -6 to 6
- east_speed: float32 [8, 1024, 2048], P(None, 'gy', 'gx'), may hold values from -0.2 to 0.2
- north_speed: float32 [8, 1024, 2048], P(None, 'gy', 'gx'), may hold values from -0.2 to 0.2
- vertical_mix: float32 [7, 1024, 2048], P(None, 'gy', 'gx'), may hold values from 0.05 to 5
- level_count: int32 [1024, 2048], P('gy', 'gx'), may hold values from 0 to 8, as said below
- atmosphere_flux: float32 [8, 256, 1024], P(None, 'gy', 'gx'), may hold values from -6 to 6
- intersection_source: int32 [8192, 1024], P('gy', 'gx'), may hold values from 0 to 2047, as said below
- intersection_target: int32 [8192, 1024], P('gy', 'gx'), may hold values from 0 to 16383, as said below
- intersection_weight: float32 [8192, 1024], P('gy', 'gx'), may hold values from 0 to 1, as said below
Outputs:
- tracers_out: float32 [2, 8, 1024, 2048], P(None, None, 'gy', 'gx')
- surface_flux: float32 [8, 1024, 2048], P(None, 'gy', 'gx')
Inputs may be any that keep to these rules, and one draw needn't show every extreme that they name: `intersection_source`: the slot from one atmosphere tile to one ocean tile of the same longitude tile has 4096 entries, live entries first. A slot from latitude tile s to latitude tile d holds live entries only where |d - s| <= 1, or where d >= 14 and s >= 7; every such slot has at least one; other slots are all padding. Padded entries have source cell 0, target cell 0 and weight 0. `intersection_target`: padded entries name cell 0. `intersection_weight`: zero on padded entries, positive on live ones. `level_count`: 0 marks land.
All inputs are finite; a program needn't handle non-finite values.
Results may differ from a plain program's by a relative error of at most 0.0003.
Values sent between devices are 32-bit elements; how exact they have to be, the bound alone decides.
No kernel may reach another device: no remote copies, remote signals or barrier semaphores. Data moves between devices by JAX's collectives and lax.ppermute only.
A program may use at most 64 MiB of HBM per device.

v0:
```python
import functools

import jax
import jax.numpy as jnp
from jax import lax
from jax.experimental import pallas as pl
from jax.experimental.pallas import tpu as pltpu
from jax.sharding import PartitionSpec as P

DIFFUSE = 0.05
FIELDS = 8
TRACERS = 2
NZ = 8
ROWS = 64
COLUMNS = 256
LANES = 128
GX = 8
GY = 16
SLOT_ROWS = 32
ATMOS_ROWS = 16
HELPERS = ((8, GY - 2), (13, GY - 1))
ENTRY_STEPS = (
    ((9, 8), (10, 13), (7, 14), (8, 15)),
    ((10, 8), (11, 13), (12, 14), (7, 15)),
    ((11, 8), (12, 13), (9, 15)),
)
HELPED_BY = {helper: target for helper, target in HELPERS}
CHANNELS = TRACERS * NZ
COUNT_AT = 24
RIM = 32
PAYLOAD = 3 * SLOT_ROWS + FIELDS * ATMOS_ROWS
CHUNK_ROWS = 16
CHUNK = CHUNK_ROWS * LANES
CHUNKS = SLOT_ROWS // CHUNK_ROWS
VMEM_LIMIT = 48 * 1024 * 1024
F32 = jnp.float32
BF16 = jnp.bfloat16
F8 = jnp.float8_e4m3fn
LOW_TOP = 65536.0


def call(kernel, out_shapes, operands, scratch=(), flops=0, moved=4_000_000, in_hbm=False):
    place = pl.ANY if in_hbm else pltpu.VMEM
    return pl.pallas_call(
        kernel,
        out_shape=[jax.ShapeDtypeStruct(shape, F32) for shape in out_shapes],
        in_specs=[pl.BlockSpec(memory_space=place) for _ in operands],
        out_specs=[pl.BlockSpec(memory_space=pltpu.VMEM) for _ in out_shapes],
        scratch_shapes=list(scratch),
        compiler_params=pltpu.CompilerParams(vmem_limit_bytes=VMEM_LIMIT),
        cost_estimate=pl.CostEstimate(flops=flops, bytes_accessed=moved, transcendentals=0),
    )(*operands)


def pack_columns(pick, channels, out_ref):
    lane = lax.broadcasted_iota(jnp.int32, (8, LANES), 1)
    for block in range(ROWS // 8):
        tile = jnp.zeros((8, LANES), F32)
        for channel in channels:
            value, at = pick(channel, block * 8)
            shift = (channel - at) % LANES
            moved = pltpu.roll(value, shift, axis=1) if shift else value
            tile = jnp.where(lane == channel, moved, tile)
        out_ref[pl.ds(block * 8, 8), :] = tile


def pack_row(value, channel, out_ref):
    out_ref[pl.ds(channel, 1), :] = value[:, :LANES]
    out_ref[pl.ds(RIM + channel, 1), :] = value[:, LANES:]


def is_even():
    return lax.rem(lax.axis_index("gy"), 2) == 0


def pack_rows(top_of, bottom_of, channels, sibling_ref, other_ref):
    even = is_even()
    zeros = jnp.zeros((2 * RIM, LANES), F32)
    sibling_ref[0 : 2 * RIM, :] = zeros
    other_ref[0 : 2 * RIM, :] = zeros
    for channel in channels:
        top, bottom = top_of(channel), bottom_of(channel)
        pack_row(jnp.where(even, top, bottom), channel, sibling_ref)
        pack_row(jnp.where(even, bottom, top), channel, other_ref)


def chosen(here, table, default):
    for key, value in table.items():
        default = jnp.where(here == key, value, default)
    return default


def pack_kernel(
    tracers_hbm,
    east_hbm,
    north_hbm,
    count_hbm,
    atmos_hbm,
    source_hbm,
    target_hbm,
    weight_hbm,
    to_east_ref,
    to_west_ref,
    sibling_ref,
    other_ref,
    first_ref,
    second_ref,
    *refs,
):
    entry_refs, scratch = refs[: len(ENTRY_STEPS)], refs[len(ENTRY_STEPS) :]
    tracers_ref, east_ref, north_ref, count_ref, atmos_ref, source_ref, target_ref, weight_ref = scratch[:8]
    sems = scratch[8]
    here = lax.axis_index("gy")
    even = is_even()
    lists = ((source_hbm, source_ref), (target_hbm, target_ref), (weight_hbm, weight_ref))
    copies = [
        *lists,
        (atmos_hbm, atmos_ref),
        (tracers_hbm, tracers_ref),
        (east_hbm.at[:, :, pl.ds(LANES, LANES)], east_ref),
        (north_hbm.at[:, pl.ds(ROWS - 8, 8), :], north_ref),
        (count_hbm, count_ref),
    ]
    copies = [
        pltpu.make_async_copy(source, into, sems.at[n]) for n, (source, into) in enumerate(copies)
    ]
    for copy in copies:
        copy.start()
    for copy in copies[:4]:
        copy.wait()

    def slot_into(out_ref, at, tile, valid=None):
        rows = pl.ds(pl.multiple_of(tile * SLOT_ROWS, SLOT_ROWS), SLOT_ROWS)
        out_ref[at : at + SLOT_ROWS, :] = source_ref[rows, :].astype(F32)
        out_ref[at + SLOT_ROWS : at + 2 * SLOT_ROWS, :] = target_ref[rows, :].astype(F32)
        weight = weight_ref[rows, :]
        if valid is not None:
            weight = jnp.where(valid, weight, 0.0)
        out_ref[at + 2 * SLOT_ROWS : at + 3 * SLOT_ROWS, :] = weight
        for field in range(FIELDS):
            for row in range(ATMOS_ROWS):
                to = at + 3 * SLOT_ROWS + row * FIELDS + field
                out_ref[to : to + 1, :] = atmos_ref[field, row : row + 1, :]

    for pairs, out_ref in zip(ENTRY_STEPS, entry_refs, strict=True):
        table = {source: HELPED_BY.get(target, target) for source, target in pairs}
        slot_into(out_ref, 0, chosen(here, table, here))
    slot_into(first_ref, 0, chosen(here, HELPED_BY, here))
    helps = functools.reduce(jnp.logical_or, [here == helper for helper in HELPED_BY])
    slot_into(second_ref, 0, here, helps)
    slot_into(sibling_ref, 2 * RIM, jnp.where(even, here + 1, here - 1))
    away = jnp.clip(jnp.where(even, here - 1, here + 1), 0, GY - 1)
    slot_into(other_ref, 2 * RIM, away, here != GY - 1)

    for copy in copies[4:]:
        copy.wait()

    def east_column(channel, row):
        rows = pl.ds(row, 8)
        if channel < CHANNELS:
            return tracers_ref[channel, rows, LANES:], LANES - 1
        if channel < COUNT_AT:
            return east_ref[channel - CHANNELS, rows, :], LANES - 1
        return count_ref[rows, LANES:].astype(F32), LANES - 1

    def west_column(channel, row):
        rows = pl.ds(row, 8)
        if channel < CHANNELS:
            return tracers_ref[channel, rows, :LANES], 0
        return count_ref[rows, :LANES].astype(F32), 0

    pack_columns(east_column, [*range(CHANNELS + NZ), COUNT_AT], to_east_ref)
    pack_columns(west_column, [*range(CHANNELS), COUNT_AT], to_west_ref)

    def top_of(channel):
        if channel < CHANNELS:
            return tracers_ref[channel, ROWS - 1 : ROWS, :]
        if channel < COUNT_AT:
            return north_ref[channel - CHANNELS, 7:8, :]
        return count_ref[ROWS - 1 : ROWS, :].astype(F32)

    def bottom_of(channel):
        if channel < CHANNELS:
            return tracers_ref[channel, 0:1, :]
        if channel < COUNT_AT:
            return jnp.zeros((1, COLUMNS), F32)
        return count_ref[0:1, :].astype(F32)

    pack_rows(top_of, bottom_of, range(COUNT_AT + 1), sibling_ref, other_ref)


def step_kernel(
    forced,
    q_ref,
    from_west_ref,
    from_east_ref,
    from_sibling_ref,
    from_other_ref,
    static_west_ref,
    static_east_ref,
    static_sibling_ref,
    static_other_ref,
    east_ref,
    north_ref,
    count_ref,
    mix_ref,
    *more_refs,
):
    if forced:
        out_ref, gain_ref = more_refs[:2]
    else:
        forcing_ref, out_ref = more_refs[:2]
    from_south_ref, top_ref, static_south_ref, static_top_ref = more_refs[2:]
    even = is_even()
    on_top = lax.axis_index("gy") == GY - 1
    lane = lax.broadcasted_iota(jnp.int32, (8, LANES), 1)
    row = lax.broadcasted_iota(jnp.int32, (8, LANES), 0)
    first_lane, last_lane = lane == 0, lane == LANES - 1
    first_row, last_row = row == 0, row == 7

    def set_rims(sibling_rim, other_rim, south, north):
        @pl.when(even)
        def _():
            south[...] = other_rim[0 : 2 * RIM, :]
            north[...] = sibling_rim[0 : 2 * RIM, :]

        @pl.when(jnp.logical_not(even))
        def _():
            south[...] = sibling_rim[0 : 2 * RIM, :]
            north[...] = other_rim[0 : 2 * RIM, :]

        @pl.when(on_top)
        def _():
            flipped = LANES - 1 - lane
            for half in range(2):
                for block in range(RIM // 8):
                    rows = other_rim[pl.ds((1 - half) * RIM + block * 8, 8), :]
                    north[pl.ds(half * RIM + block * 8, 8), :] = jnp.take_along_axis(
                        rows, flipped, axis=1, mode="promise_in_bounds"
                    )

    set_rims(from_sibling_ref, from_other_ref, from_south_ref, top_ref)
    set_rims(static_sibling_ref, static_other_ref, static_south_ref, static_top_ref)

    def block_step(block, carry):
        at = pl.multiple_of(block * 8, 8)
        below = pl.multiple_of(jnp.maximum(block - 1, 0) * 8, 8)
        above = pl.multiple_of(jnp.minimum(block + 1, ROWS // 8 - 1) * 8, 8)
        is_first, is_last = block == 0, block == ROWS // 8 - 1
        rows = pl.ds(at, 8)

        def halves(load):
            return [load(rows, slice(0, LANES)), load(rows, slice(LANES, 2 * LANES))]

        def to_west_of(parts, rim):
            low = jnp.where(last_lane, rim, parts[0])
            high = jnp.where(last_lane, parts[0], parts[1])
            return [pltpu.roll(low, 1, axis=1), pltpu.roll(high, 1, axis=1)]

        def to_east_of(parts, rim):
            low = jnp.where(first_lane, parts[1], parts[0])
            high = jnp.where(first_lane, rim, parts[1])
            return [
                pltpu.roll(low, LANES - 1, axis=1),
                pltpu.roll(high, LANES - 1, axis=1),
            ]

        def to_south_of(load, parts, rim_ref, channel):
            found = []
            for half in range(2):
                lanes = slice(half * LANES, (half + 1) * LANES)
                rim = jnp.broadcast_to(
                    rim_ref[half * RIM + channel : half * RIM + channel + 1, :], (8, LANES)
                )
                near = jnp.where(is_first, rim, load(pl.ds(below, 8), lanes))
                found.append(pltpu.roll(jnp.where(last_row, near, parts[half]), 1, axis=0))
            return found

        def to_north_of(load, parts, rim_ref, channel):
            found = []
            for half in range(2):
                lanes = slice(half * LANES, (half + 1) * LANES)
                rim = jnp.broadcast_to(
                    rim_ref[half * RIM + channel : half * RIM + channel + 1, :], (8, LANES)
                )
                near = jnp.where(is_last, rim, load(pl.ds(above, 8), lanes))
                found.append(pltpu.roll(jnp.where(first_row, near, parts[half]), 7, axis=0))
            return found

        def west_rim(ref, channel):
            return pltpu.roll(ref[rows, :], (LANES - 1 - channel) % LANES, axis=1)

        def east_rim(ref, channel):
            shift = (LANES - channel) % LANES
            return pltpu.roll(ref[rows, :], shift, axis=1) if shift else ref[rows, :]

        def load_count(where, lanes):
            return count_ref[where, lanes].astype(F32)

        count = halves(load_count)
        sides = [
            to_east_of(count, east_rim(static_east_ref, COUNT_AT)),
            to_west_of(count, west_rim(static_west_ref, COUNT_AT)),
            to_north_of(load_count, count, static_top_ref, COUNT_AT),
            to_south_of(load_count, count, static_south_ref, COUNT_AT),
        ]
        shared = [[jnp.minimum(count[half], side[half]) for half in range(2)] for side in sides]
        closed = jnp.logical_and(jnp.logical_and(on_top, is_last), last_row)

        values = [[[None, None] for _ in range(NZ)] for _ in range(TRACERS)]
        for level in range(NZ):
            east = halves(lambda where, lanes: east_ref[level, where, lanes])
            west = to_west_of(east, west_rim(static_west_ref, CHANNELS + level))

            def load_north(where, lanes):
                return north_ref[level, where, lanes]

            north = halves(load_north)
            south = to_south_of(load_north, north, static_south_ref, CHANNELS + level)
            coefs = []
            for half in range(2):
                limit = float(level)
                up = jnp.where(closed, 0.0, north[half])
                open_e, open_w, open_n, open_s = [side[half] > limit for side in shared]

                def into(opened, speed):
                    return jnp.where(opened, DIFFUSE - jnp.minimum(speed, 0.0), 0.0)

                def away(opened, speed):
                    return jnp.where(opened, DIFFUSE + jnp.maximum(speed, 0.0), 0.0)

                from_e, lost_e = into(open_e, east[half]), away(open_e, east[half])
                from_w, lost_w = away(open_w, west[half]), into(open_w, west[half])
                from_n, lost_n = into(open_n, up), away(open_n, up)
                from_s, lost_s = away(open_s, south[half]), into(open_s, south[half])
                kept = 1.0 - ((lost_e + lost_w) + (lost_n + lost_s))
                coefs.append((kept, from_e, from_w, from_n, from_s))
            for tracer in range(TRACERS):
                channel = tracer * NZ + level

                def load_q(where, lanes):
                    return q_ref[channel, where, lanes]

                q = halves(load_q)
                q_e = to_east_of(q, east_rim(from_east_ref, channel))
                q_w = to_west_of(q, west_rim(from_west_ref, channel))
                q_n = to_north_of(load_q, q, top_ref, channel)
                q_s = to_south_of(load_q, q, from_south_ref, channel)
                for half in range(2):
                    kept, from_e, from_w, from_n, from_s = coefs[half]
                    values[tracer][level][half] = (
                        kept * q[half]
                        + (from_e * q_e[half] + from_w * q_w[half])
                        + (from_n * q_n[half] + from_s * q_s[half])
                    )
        for half in range(2):
            lanes = slice(half * LANES, (half + 1) * LANES)
            sides_here = [[values[t][k][half] for k in range(NZ)] for t in range(TRACERS)]
            surface = count[half] > 0.0
            if forced:
                sides_here.append([jnp.where(surface, 1.0, 0.0)] + [None] * (NZ - 1))
            else:
                for tracer in range(TRACERS):
                    forcing = jnp.where(surface, forcing_ref[tracer, rows, lanes], 0.0)
                    sides_here[tracer][0] = sides_here[tracer][0] + forcing
            ratios = []
            partials = [[] for _ in sides_here]
            for level in range(NZ):
                thickness = 1.0 + level / NZ
                upper = lower = None
                if level >= 1:
                    mix = mix_ref[level - 1, rows, lanes]
                    upper = jnp.where(count[half] > float(level), mix * (1.0 / thickness), 0.0)
                if level <= NZ - 2:
                    mix = mix_ref[level, rows, lanes]
                    lower = jnp.where(
                        count[half] > float(level + 1), mix * (1.0 / thickness), 0.0
                    )
                if upper is None:
                    pivot = 1.0 + lower
                elif lower is None:
                    pivot = 1.0 + upper - upper * ratios[-1]
                else:
                    pivot = 1.0 + upper + lower - upper * ratios[-1]
                inverse = 1.0 / pivot
                if lower is not None:
                    ratios.append(lower * inverse)
                for side, partial in zip(sides_here, partials, strict=True):
                    right = side[level]
                    if level >= 1:
                        carried = upper * partial[-1]
                        right = carried if right is None else right + carried
                    partial.append(right * inverse)
            for index, partial in enumerate(partials):
                solved = partial[-1]
                for level in range(NZ - 1, -1, -1):
                    if level < NZ - 1:
                        solved = partial[level] + ratios[level] * solved
                    if index < TRACERS:
                        out_ref[index * NZ + level, rows, lanes] = solved
                    else:
                        gain_ref[level, rows, lanes] = solved
        return carry

    lax.fori_loop(0, ROWS // 8, block_step, 0)


def land_kernel(offsets, continued, *refs):
    slot_refs, refs = refs[: len(offsets)], refs[len(offsets) :]
    if continued:
        start_ref, refs = refs[0], refs[1:]
    total_ref, lists_ref, cells_ref, high_ref, low_ref, high_hot_ref, low_hot_ref, live_ref = refs
    largest = jnp.zeros((8, LANES), F32)
    for slot, (ref, at) in enumerate(zip(slot_refs, offsets, strict=True)):
        for kind in range(3):
            rows = pl.ds(at + kind * SLOT_ROWS, SLOT_ROWS)
            lists_ref[kind, pl.ds(slot * SLOT_ROWS, SLOT_ROWS), :] = ref[rows, :]
        for row in range(ATMOS_ROWS):
            cells = ref[pl.ds(at + 3 * SLOT_ROWS + row * FIELDS, FIELDS), :]
            cells_ref[slot, row] = cells
            largest = jnp.maximum(largest, jnp.abs(cells))
    scale = LOW_TOP / jnp.maximum(jnp.max(largest), 1e-30)
    unscale = 1.0 / scale

    found = jnp.int32(0)
    for index in range(len(offsets) * CHUNKS):
        weights = lists_ref[2, pl.ds(index * CHUNK_ROWS, CHUNK_ROWS), :]
        live_ref[found] = index
        found = found + (jnp.max(weights) > 0.0).astype(jnp.int32)

    if continued:
        helps = functools.reduce(
            jnp.logical_or, [lax.axis_index("gy") == helper for helper in HELPED_BY]
        )

        @pl.when(helps)
        def _():
            total_ref[...] = jnp.zeros_like(total_ref)

        @pl.when(jnp.logical_not(helps))
        def _():
            total_ref[...] = start_ref[...]
    else:
        total_ref[...] = jnp.zeros_like(total_ref)
    ones, zeros = jnp.ones((), BF16), jnp.zeros((), BF16)
    iota = lax.broadcasted_iota(jnp.int32, (COLUMNS, LANES), 0).astype(F32).astype(BF16)

    def hot(values, entry, count):
        line = jnp.broadcast_to(values[entry : entry + 1, :], (16, LANES)).astype(BF16)
        return [jnp.where(line == iota[at : at + 16], ones, zeros) for at in range(0, count, 16)]

    def chunk_step(at, carry):
        index = live_ref[at]
        slot = lax.div(index, CHUNKS)
        rows = pl.ds(pl.multiple_of(index * CHUNK_ROWS, CHUNK_ROWS), CHUNK_ROWS)
        source, target, weight = lists_ref[0, rows, :], lists_ref[1, rows, :], lists_ref[2, rows, :]
        source_row = jnp.floor(source * (1.0 / LANES))
        source_column = (source - source_row * LANES).astype(jnp.int32)
        target_row = jnp.floor(target * (1.0 / COLUMNS))
        target_column = target - target_row * COLUMNS
        for entry in range(CHUNK_ROWS):
            lanes = slice(entry * LANES, (entry + 1) * LANES)
            row_here = jnp.broadcast_to(source_row[entry : entry + 1, :], (FIELDS, LANES))
            column_here = jnp.broadcast_to(source_column[entry : entry + 1, :], (FIELDS, LANES))
            picked = jnp.zeros((FIELDS, LANES), F32)
            for row in range(ATMOS_ROWS):
                found_here = jnp.take_along_axis(
                    cells_ref[slot, row], column_here, axis=1, mode="promise_in_bounds"
                )
                picked = jnp.where(row_here == float(row), found_here, picked)
            weighted = picked * weight[entry : entry + 1, :]
            high = weighted.astype(BF16).astype(F32)
            low = (weighted - high) * scale
            row_hot = hot(target_row, entry, ROWS)
            for field in range(FIELDS):
                first = field * ROWS
                line = jnp.broadcast_to(high[field : field + 1, :], (16, LANES)).astype(BF16)
                for part in range(4):
                    high_ref[first + part * 16 : first + part * 16 + 16, lanes] = line * row_hot[part]
                line = jnp.broadcast_to(low[field : field + 1, :], (16, LANES)).astype(BF16)
                for part in range(2):
                    both = [line * row_hot[2 * part], line * row_hot[2 * part + 1]]
                    low_ref[first + part * 32 : first + part * 32 + 32, lanes] = jnp.concatenate(
                        both, axis=0
                    ).astype(F8)
            column_hot = hot(target_column, entry, COLUMNS)
            for part in range(COLUMNS // 16):
                high_hot_ref[part * 16 : part * 16 + 16, lanes] = column_hot[part]
            for part in range(COLUMNS // 32):
                low_hot_ref[part * 32 : part * 32 + 32, lanes] = jnp.concatenate(
                    column_hot[2 * part : 2 * part + 2], axis=0
                ).astype(F8)
        over_entries = (((1,), (1,)), ((), ()))
        total_ref[...] += lax.dot_general(
            high_ref[...], high_hot_ref[...], over_entries, preferred_element_type=F32
        ) + unscale * lax.dot_general(
            low_ref[...], low_hot_ref[...], over_entries, preferred_element_type=F32
        )
        return carry

    lax.fori_loop(0, found, chunk_step, 0)


def finish_kernel(
    total_ref,
    helped_ref,
    solved_ref,
    gain_ref,
    result_ref,
    flux_ref,
    forcing_ref,
    to_east_ref,
    to_west_ref,
    sibling_ref,
    other_ref,
):
    def block_step(block, carry):
        rows = pl.ds(pl.multiple_of(block * 8, 8), 8)
        flux = []
        for field in range(FIELDS):
            from_rows = pl.ds(pl.multiple_of(field * ROWS + block * 8, 8), 8)
            value = total_ref[from_rows, :] + helped_ref[from_rows, :]
            flux_ref[field, rows, :] = value
            flux.append(value)
        heat = flux[0] + flux[1] + flux[2] + flux[3] + flux[4]
        salt = flux[7] - flux[5] - flux[6]
        forcing_ref[0, rows, :] = heat
        forcing_ref[1, rows, :] = salt
        for level in range(NZ):
            gain = gain_ref[level, rows, :]
            for tracer, forcing in enumerate((heat, salt)):
                channel = tracer * NZ + level
                result_ref[channel, rows, :] = solved_ref[channel, rows, :] + forcing * gain
        return carry

    lax.fori_loop(0, ROWS // 8, block_step, 0)
    pack_columns(
        lambda channel, row: (result_ref[channel, pl.ds(row, 8), LANES:], LANES - 1),
        range(CHANNELS),
        to_east_ref,
    )
    pack_columns(
        lambda channel, row: (result_ref[channel, pl.ds(row, 8), :LANES], 0),
        range(CHANNELS),
        to_west_ref,
    )
    pack_rows(
        lambda channel: result_ref[channel, ROWS - 1 : ROWS, :],
        lambda channel: result_ref[channel, 0:1, :],
        range(CHANNELS),
        sibling_ref,
        other_ref,
    )


EASTWARD = [(i, (i + 1) % GX) for i in range(GX)]
WESTWARD = [((i + 1) % GX, i) for i in range(GX)]
SIBLINGS = [(y, y ^ 1) for y in range(GY)]
OTHERS = [
    (x * GY + y, x * GY + (y + 1 if y % 2 else y - 1)) for x in range(GX) for y in range(1, GY - 1)
] + [(x * GY + GY - 1, (GX - 1 - x) * GY + GY - 1) for x in range(GX)]


def exchange(to_east, to_west, sibling, other):
    return (
        lax.ppermute(to_east, "gx", EASTWARD),
        lax.ppermute(to_west, "gx", WESTWARD),
        lax.ppermute(sibling, "gy", SIBLINGS),
        lax.ppermute(other, ("gx", "gy"), OTHERS),
    )


def land(slots, offsets, start=()):
    count = len(slots)
    (total,) = call(
        functools.partial(land_kernel, offsets, bool(start)),
        [(FIELDS * ROWS, COLUMNS)],
        [*slots, *start],
        [
            pltpu.VMEM((3, count * SLOT_ROWS, LANES), F32),
            pltpu.VMEM((count, ATMOS_ROWS, FIELDS, LANES), F32),
            pltpu.VMEM((FIELDS * ROWS, CHUNK), BF16),
            pltpu.VMEM((FIELDS * ROWS, CHUNK), F8),
            pltpu.VMEM((COLUMNS, CHUNK), BF16),
            pltpu.VMEM((COLUMNS, CHUNK), F8),
            pltpu.SMEM((count * CHUNKS + 1,), jnp.int32),
        ],
        flops=4_000_000_000,
        moved=20_000_000,
    )
    return total


def local(
    tracers,
    east_speed,
    north_speed,
    vertical_mix,
    level_count,
    atmosphere_flux,
    intersection_source,
    intersection_target,
    intersection_weight,
):
    q = tracers.reshape(CHANNELS, ROWS, COLUMNS)
    lists = [intersection_source, intersection_target, intersection_weight]
    column_rim, row_rim = (ROWS, LANES), (2 * RIM, LANES)
    near, slot = (2 * RIM + PAYLOAD, LANES), (PAYLOAD, LANES)
    steps = len(ENTRY_STEPS)
    to_east, to_west, sibling, other, first, second, *entries = call(
        pack_kernel,
        [column_rim, column_rim, near, near] + [slot] * (2 + steps),
        [q, east_speed, north_speed, level_count, atmosphere_flux, *lists],
        [
            pltpu.VMEM(q.shape, F32),
            pltpu.VMEM((NZ, ROWS, LANES), F32),
            pltpu.VMEM((NZ, 8, COLUMNS), F32),
            pltpu.VMEM(level_count.shape, jnp.int32),
            pltpu.VMEM(atmosphere_flux.shape, F32),
            *[pltpu.VMEM(part.shape, part.dtype) for part in lists],
            pltpu.SemaphoreType.DMA((8,)),
        ],
        in_hbm=True,
    )
    entries = [
        lax.ppermute(part, "gy", list(pairs))
        for part, pairs in zip(entries, ENTRY_STEPS, strict=True)
    ]
    rims = exchange(to_east, to_west, sibling, other)
    partial = land([first, *entries], (0,) * (1 + steps))
    helped = lax.ppermute(partial, "gy", list(HELPERS))
    total = land([second, rims[2], rims[3]], (0, 2 * RIM, 2 * RIM), (partial,))
    statics = [east_speed, north_speed, level_count, vertical_mix]
    rim_scratch = [pltpu.VMEM(row_rim, F32)] * 4
    solved, gain = call(
        functools.partial(step_kernel, True),
        [q.shape, east_speed.shape],
        [q, *rims, *rims, *statics],
        rim_scratch,
        moved=8_000_000,
    )
    result, flux, forcing, *out_rims = call(
        finish_kernel,
        [q.shape, (FIELDS, ROWS, COLUMNS), (TRACERS, ROWS, COLUMNS)]
        + [column_rim, column_rim, row_rim, row_rim],
        [total, helped, solved, gain],
    )
    second_rims = exchange(*out_rims)
    (result,) = call(
        functools.partial(step_kernel, False),
        [q.shape],
        [result, *second_rims, *rims, *statics, forcing],
        rim_scratch,
        moved=8_000_000,
    )
    return result.reshape(tracers.shape), flux


def solution(mesh):
    in_specs = (
        P(None, None, "gy", "gx"),
        P(None, "gy", "gx"),
        P(None, "gy", "gx"),
        P(None, "gy", "gx"),
        P("gy", "gx"),
        P(None, "gy", "gx"),
        P("gy", "gx"),
        P("gy", "gx"),
        P("gy", "gx"),
    )
    out_specs = (P(None, None, "gy", "gx"), P(None, "gy", "gx"))
    return jax.shard_map(local, mesh=mesh, in_specs=in_specs, out_specs=out_specs, check_vma=False)
```

profile of v0, /device:TPU:32, one launch (start us, length us, event | category | flops | bytes accessed | tf_op | source)
XLA Modules:
  0.0 70.9 jit_solution(8547838775558070641)
XLA Ops:
  0.6 0.0 copy-start
  0.6 1.0 %copy-done = f32[8,64,256]{2,1,0:T(8,128)S(1)} copy-done((f32[8,64,256]{2,1,0:T(8,128)S(1)}, f32[8,64,256]{2,1,0:T(8,128)}, u32[]{:S(2)}) %copy-start) | copy-done | bytes 524312
  1.7 0.0 copy-start.2
  1.7 1.0 %copy-done.2 = f32[8,64,256]{2,1,0:T(8,128)S(1)} copy-done((f32[8,64,256]{2,1,0:T(8,128)S(1)}, f32[8,64,256]{2,1,0:T(8,128)}, u32[]{:S(2)}) %copy-start.2) | copy-done | bytes 524312
  2.7 1.2 %copy-done.4 = f32[2,8,64,256]{3,2,1,0:T(8,128)S(1)} copy-done((f32[2,8,64,256]{3,2,1,0:T(8,128)S(1)}, f32[2,8,64,256]{3,2,1,0:T(8,128)}, u32[]{:S(2)}) %copy-start.4) | copy-done | bytes 1048600
  3.9 0.8 %copy-done.7 = s32[64,256]{1,0:T(8,128)S(1)} copy-done((s32[64,256]{1,0:T(8,128)S(1)}, s32[64,256]{1,0:T(8,128)}, u32[]{:S(2)}) %copy-start.7) | copy-done | bytes 65560
  4.8 0.9 %copy-done.9 = s32[512,128]{1,0:T(8,128)S(1)} copy-done((s32[512,128]{1,0:T(8,128)S(1)}, s32[512,128]{1,0:T(8,128)}, u32[]{:S(2)}) %copy-start.9) | copy-done | bytes 262168
  5.7 0.9 %copy-done.10 = s32[512,128]{1,0:T(8,128)S(1)} copy-done((s32[512,128]{1,0:T(8,128)S(1)}, s32[512,128]{1,0:T(8,128)}, u32[]{:S(2)}) %copy-start.10) | copy-done | bytes 262168
  6.7 0.9 %copy-done.11 = f32[512,128]{1,0:T(8,128)S(1)} copy-done((f32[512,128]{1,0:T(8,128)S(1)}, f32[512,128]{1,0:T(8,128)}, u32[]{:S(2)}) %copy-start.11) | copy-done | bytes 262168
  7.6 0.8 %copy-done.12 = f32[8,16,128]{2,1,0:T(8,128)S(1)} copy-done((f32[8,16,128]{2,1,0:T(8,128)S(1)}, f32[8,16,128]{2,1,0:T(8,128)}, u32[]{:S(2)}) %copy-start.12) | copy-done | bytes 65560
  8.5 1.1 %shard_map.104 = (f32[64,128]{1,0:T(8,128)S(1)}, f32[64,128]{1,0:T(8,128)S(1)}, f32[288,128]{1,0:T(8,128)S(1)}, f32[288,128]{1,0:T(8,128)S(1)}, f32[224,128]{1,0...) custom-call(f32[16,64,256]{2,1,0:T(8,128)S(1)} %bitcast.2, ...), custom_call_target="tpu_custom_call" | custom-call | bytes 4000000 | tf_op jit(solution)/shard_map/pallas_call | solution.py:44
  9.6 4.4 %collective-permute-start.2 = (f32[224,128]{1,0:T(8,128)S(1)}, f32[224,128]{1,0:T(8,128)S(1)}, u32[]{:S(2)}, u32[]{:S(2)}) collective-permute-start(f32[224,128]{1,0:T(8,128)S(1)} %get-tuple-element.24), channel_id=1, source_target_pairs={{9,8},{10,13},{7,14},{8,15},{25,24},{26,29},{23,30},{24,31},{41,40... | collective-permute-start | bytes 344072 | tf_op jit(solution)/shard_map/ppermute | solution.py:626
  14.0 1.3 %collective-permute-start.3 = (f32[224,128]{1,0:T(8,128)S(1)}, f32[224,128]{1,0:T(8,128)S(1)}, u32[]{:S(2)}, u32[]{:S(2)}) collective-permute-start(f32[224,128]{1,0:T(8,128)S(1)} %get-tuple-element.25), channel_id=1, source_target_pairs={{10,8},{11,13},{12,14},{7,15},{26,24},{27,29},{28,30},{23,31},{42,... | collective-permute-start | bytes 344072 | tf_op jit(solution)/shard_map/ppermute | solution.py:626
  15.3 1.3 %collective-permute-start.4 = (f32[224,128]{1,0:T(8,128)S(1)}, f32[224,128]{1,0:T(8,128)S(1)}, u32[]{:S(2)}, u32[]{:S(2)}) collective-permute-start(f32[224,128]{1,0:T(8,128)S(1)} %get-tuple-element.26), channel_id=1, source_target_pairs={{11,8},{12,13},{9,15},{27,24},{28,29},{25,31},{43,40},{44,45},{41,... | collective-permute-start | bytes 344072 | tf_op jit(solution)/shard_map/ppermute | solution.py:626
  16.6 0.0 collective-permute-done.2.refs_1_
  16.6 4.6 %collective-permute-done.3.refs_2_ = f32[224,128]{1,0:T(8,128)S(1)} collective-permute-done((f32[224,128]{1,0:T(8,128)S(1)}, f32[224,128]{1,0:T(8,128)S(1)}, u32[]{:S(2)}, u32[]{:S(2)}) %collective-permute-start.3) | collective-permute-done | bytes 114720 | tf_op jit(solution)/shard_map/ppermute | solution.py:626
  21.2 0.7 collective-permute-done.4.refs_3_
  21.9 8.0 %shard_map.105.refs_3_ = f32[512,256]{1,0:T(8,128)S(1)} custom-call(f32[224,128]{1,0:T(8,128)S(1)} %get-tuple-element.23.refs_0_, f32[224,128]{1,0:T(8,128)S(1)} %collective-permute-done.2.refs_1_, f32[224,128]{1,0:T(8,128)S(1)} %collective-permute-done.3.refs_2_, f32[224,128]{1,0:T(8,128)S(1)} %collective-permute-done.4.refs_3_), custom_call_target="tpu_custom_call" | custom-call | flops 4000000000 | bytes 20000000 | tf_op jit(solution)/shard_map/pallas_call | solution.py:44
  29.8 1.3 %collective-permute-start.5 = (f32[512,256]{1,0:T(8,128)S(1)}, f32[512,256]{1,0:T(8,128)S(1)}, u32[]{:S(2)}, u32[]{:S(2)}) collective-permute-start(f32[512,256]{1,0:T(8,128)S(1)} %shard_map.105.refs_3_), channel_id=1, source_target_pairs={{8,14},{13,15},{24,30},{29,31},{40,46},{45,47},{56,62},{61,63},{72... | collective-permute-start | bytes 1572872 | tf_op jit(solution)/shard_map/ppermute | solution.py:631
  31.2 0.1 collective-permute-start
  31.3 1.9 %collective-permute-start.1 = (f32[288,128]{1,0:T(8,128)S(1)}, f32[288,128]{1,0:T(8,128)S(1)}, u32[]{:S(2)}, u32[]{:S(2)}) collective-permute-start(f32[288,128]{1,0:T(8,128)S(1)} %get-tuple-element.22), channel_id=1, source_target_pairs={{1,2},{2,1},{3,4},{4,3},{5,6},{6,5},{7,8},{8,7},{9,10},{10,9},{11,... | collective-permute-start | bytes 442376 | tf_op jit(solution)/shard_map/ppermute | solution.py:569
  33.2 1.6 %collective-permute-start.6 = (f32[64,128]{1,0:T(8,128)S(1)}, f32[64,128]{1,0:T(8,128)S(1)}, u32[]{:S(2)}, u32[]{:S(2)}) collective-permute-start(f32[64,128]{1,0:T(8,128)S(1)} %get-tuple-element.27), channel_id=1, source_target_pairs={{0,16},{16,32},{32,48},{48,64},{64,80},{80,96},{96,112},{112,0},{1... | collective-permute-start | bytes 98312 | tf_op jit(solution)/shard_map/ppermute | solution.py:566
  34.7 6.3 %collective-permute-start.7 = (f32[64,128]{1,0:T(8,128)S(1)}, f32[64,128]{1,0:T(8,128)S(1)}, u32[]{:S(2)}, u32[]{:S(2)}) collective-permute-start(f32[64,128]{1,0:T(8,128)S(1)} %get-tuple-element.28), channel_id=1, source_target_pairs={{16,0},{32,16},{48,32},{64,48},{80,64},{96,80},{112,96},{0,112},{1... | collective-permute-start | bytes 98312 | tf_op jit(solution)/shard_map/ppermute | solution.py:567
  41.1 2.0 %collective-permute-done.6.from_west_ref.static_west_ref = f32[64,128]{1,0:T(8,128)S(1)} collective-permute-done((f32[64,128]{1,0:T(8,128)S(1)}, f32[64,128]{1,0:T(8,128)S(1)}, u32[]{:S(2)}, u32[]{:S(2)}) %collective-permute-start.6) | collective-permute-done | bytes 32800 | tf_op jit(solution)/shard_map/ppermute | solution.py:566
  43.0 0.0 collective-permute-done.7.from_east_ref.static_east_ref
  43.0 0.0 collective-permute-done.refs_1_.from_sibling_ref.static_sibling_ref
  43.0 0.0 collective-permute-done.1.refs_2_.from_other_ref.static_other_ref
  43.0 0.0 copy-done.5
  43.1 0.0 copy-done.6
  43.1 2.3 %shard_map.107 = (f32[16,64,256]{2,1,0:T(8,128)S(1)}, f32[8,64,256]{2,1,0:T(8,128)S(1)}) custom-call(f32[16,64,256]{2,1,0:T(8,128)S(1)} %bitcast.3, f32[64,128]{1,0:T(8,128)S(1)} %collective-permute-done.6.from_west_ref.static_west_ref, f32[64,128]{1,0:T(8,128)S(1)} %collective-permute-done.7.from_east_ref.static_east_ref, ...), custom_call_target="tpu_custom_call" | custom-call | bytes 8000000 | tf_op jit(solution)/shard_map/pallas_call | solution.py:44
  45.3 8.0 %shard_map.106.total_ref = f32[512,256]{1,0:T(8,128)S(1)} custom-call(f32[224,128]{1,0:T(8,128)S(1)} %get-tuple-element.20.refs_0_, f32[288,128]{1,0:T(8,128)S(1)} %collective-permute-done.refs_1_.from_sibling_ref.static_sibling_ref, f32[288,128]{1,0:T(8,128)S(1)} %collective-permute-done.1.refs_2_.from_other_ref.static_other_ref, ...), custom_call_target="tpu_custom_call" | custom-call | flops 4000000000 | bytes 20000000 | tf_op jit(solution)/shard_map/pallas_call | solution.py:44
  53.3 0.0 collective-permute-done.5.helped_ref
  53.3 0.0 copy-start.1
  53.3 0.0 copy-start.3
  53.4 0.0 copy-start.8
  53.4 1.3 %shard_map.108 = (f32[16,64,256]{2,1,0:T(8,128)S(1)}, f32[8,64,256]{2,1,0:T(8,128)}, f32[2,64,256]{2,1,0:T(8,128)S(1)}, f32[64,128]{1,0:T(8,128)S(1)}, f32[64,12...) custom-call(f32[512,256]{1,0:T(8,128)S(1)} %shard_map.106.total_ref, ...), custom_call_target="tpu_custom_call" | custom-call | bytes 4000000 | tf_op jit(solution)/shard_map/pallas_call | solution.py:44
  54.7 0.0 collective-permute-start.8
  54.7 5.6 %collective-permute-start.9 = (f32[64,128]{1,0:T(8,128)S(1)}, f32[64,128]{1,0:T(8,128)S(1)}, u32[]{:S(2)}, u32[]{:S(2)}) collective-permute-start(f32[64,128]{1,0:T(8,128)S(1)} %get-tuple-element.33), channel_id=1, source_target_pairs={{16,0},{32,16},{48,32},{64,48},{80,64},{96,80},{112,96},{0,112},{1... | collective-permute-start | bytes 98312 | tf_op jit(solution)/shard_map/ppermute | solution.py:567
  60.3 0.0 collective-permute-start.10
  60.3 1.9 %collective-permute-start.11 = (f32[64,128]{1,0:T(8,128)S(1)}, f32[64,128]{1,0:T(8,128)S(1)}, u32[]{:S(2)}, u32[]{:S(2)}) collective-permute-start(f32[64,128]{1,0:T(8,128)S(1)} %get-tuple-element.35), channel_id=1, source_target_pairs={{1,2},{2,1},{3,4},{4,3},{5,6},{6,5},{7,8},{8,7},{9,10},{10,9},{11,... | collective-permute-start | bytes 98312 | tf_op jit(solution)/shard_map/ppermute | solution.py:569
  62.2 0.0 collective-permute-done.8.from_west_ref
  62.2 0.0 collective-permute-done.9.from_east_ref
  62.3 0.0 collective-permute-done.10.from_sibling_ref
  62.3 5.4 %collective-permute-done.11.from_other_ref = f32[64,128]{1,0:T(8,128)S(1)} collective-permute-done((f32[64,128]{1,0:T(8,128)S(1)}, f32[64,128]{1,0:T(8,128)S(1)}, u32[]{:S(2)}, u32[]{:S(2)}) %collective-permute-start.11) | collective-permute-done | bytes 32800 | tf_op jit(solution)/shard_map/ppermute | solution.py:569
  67.6 0.0 copy-done.1
  67.7 0.0 copy-done.3
  67.7 0.0 copy-done.8
  67.7 3.2 %shard_map.109 = f32[16,64,256]{2,1,0:T(8,128)} custom-call(f32[16,64,256]{2,1,0:T(8,128)S(1)} %get-tuple-element.31.q_ref, f32[64,128]{1,0:T(8,128)S(1)} %collective-permute-done.8.from_west_ref, f32[64,128]{1,0:T(8,128)S(1)} %collective-permute-done.9.from_east_ref, f32[64,128]{1,0:T(8,128)S(1)} %collective-permute-done.10.from_sibling_ref, ...), custom_call_target="tpu_custom_call" | custom-call | bytes 8000000 | tf_op jit(solution)/shard_map/pallas_call | solution.py:44
  (8 shorter events, 0.0 us)
Async XLA Ops:
  0.6 1.0 %copy-start = (f32[8,64,256]{2,1,0:T(8,128)S(1)}, f32[8,64,256]{2,1,0:T(8,128)}, u32[]{:S(2)}) copy-start(f32[8,64,256]{2,1,0:T(8,128)} %east_ref.3) | copy-start | bytes 1572868
  1.7 1.0 %copy-start.2 = (f32[8,64,256]{2,1,0:T(8,128)S(1)}, f32[8,64,256]{2,1,0:T(8,128)}, u32[]{:S(2)}) copy-start(f32[8,64,256]{2,1,0:T(8,128)} %north_ref.3) | copy-start | bytes 1572868
  2.7 1.2 %copy-start.4 = (f32[2,8,64,256]{3,2,1,0:T(8,128)S(1)}, f32[2,8,64,256]{3,2,1,0:T(8,128)}, u32[]{:S(2)}) copy-start(f32[2,8,64,256]{3,2,1,0:T(8,128)} %param.9) | copy-start | bytes 3145732
  3.9 0.8 %copy-start.7 = (s32[64,256]{1,0:T(8,128)S(1)}, s32[64,256]{1,0:T(8,128)}, u32[]{:S(2)}) copy-start(s32[64,256]{1,0:T(8,128)} %count_ref.3) | copy-start | bytes 196612
  4.8 0.9 %copy-start.9 = (s32[512,128]{1,0:T(8,128)S(1)}, s32[512,128]{1,0:T(8,128)}, u32[]{:S(2)}) copy-start(s32[512,128]{1,0:T(8,128)} %source_hbm.1) | copy-start | bytes 786436
  5.7 0.9 %copy-start.10 = (s32[512,128]{1,0:T(8,128)S(1)}, s32[512,128]{1,0:T(8,128)}, u32[]{:S(2)}) copy-start(s32[512,128]{1,0:T(8,128)} %target_hbm.1) | copy-start | bytes 786436
  6.7 0.9 %copy-start.11 = (f32[512,128]{1,0:T(8,128)S(1)}, f32[512,128]{1,0:T(8,128)}, u32[]{:S(2)}) copy-start(f32[512,128]{1,0:T(8,128)} %weight_hbm.1) | copy-start | bytes 786436
  7.6 0.8 %copy-start.12 = (f32[8,16,128]{2,1,0:T(8,128)S(1)}, f32[8,16,128]{2,1,0:T(8,128)}, u32[]{:S(2)}) copy-start(f32[8,16,128]{2,1,0:T(8,128)} %atmos_hbm.1) | copy-start | bytes 196612
  9.6 7.0 %collective-permute-start.2 = (f32[224,128]{1,0:T(8,128)S(1)}, f32[224,128]{1,0:T(8,128)S(1)}, u32[]{:S(2)}, u32[]{:S(2)}) collective-permute-start(f32[224,128]{1,0:T(8,128)S(1)} %get-tuple-element.24), channel_id=1, source_target_pairs={{9,8},{10,13},{7,14},{8,15},{25,24},{26,29},{23,30},{24,31},{41,40... | collective-permute-start | bytes 344072 | tf_op jit(solution)/shard_map/ppermute | solution.py:626
  14.0 7.2 %collective-permute-start.3 = (f32[224,128]{1,0:T(8,128)S(1)}, f32[224,128]{1,0:T(8,128)S(1)}, u32[]{:S(2)}, u32[]{:S(2)}) collective-permute-start(f32[224,128]{1,0:T(8,128)S(1)} %get-tuple-element.25), channel_id=1, source_target_pairs={{10,8},{11,13},{12,14},{7,15},{26,24},{27,29},{28,30},{23,31},{42,... | collective-permute-start | bytes 344072 | tf_op jit(solution)/shard_map/ppermute | solution.py:626
  15.3 6.6 %collective-permute-start.4 = (f32[224,128]{1,0:T(8,128)S(1)}, f32[224,128]{1,0:T(8,128)S(1)}, u32[]{:S(2)}, u32[]{:S(2)}) collective-permute-start(f32[224,128]{1,0:T(8,128)S(1)} %get-tuple-element.26), channel_id=1, source_target_pairs={{11,8},{12,13},{9,15},{27,24},{28,29},{25,31},{43,40},{44,45},{41,... | collective-permute-start | bytes 344072 | tf_op jit(solution)/shard_map/ppermute | solution.py:626
  21.9 21.2 %copy-start.5 = (f32[2,8,64,256]{3,2,1,0:T(8,128)S(1)}, f32[2,8,64,256]{3,2,1,0:T(8,128)}, u32[]{:S(2)}) copy-start(f32[2,8,64,256]{3,2,1,0:T(8,128)} %param.9) | copy-start | bytes 3145732
  21.9 21.2 %copy-start.6 = (f32[7,64,256]{2,1,0:T(8,128)S(1)}, f32[7,64,256]{2,1,0:T(8,128)}, u32[]{:S(2)}) copy-start(f32[7,64,256]{2,1,0:T(8,128)} %mix_ref.3) | copy-start | bytes 1376260
  29.8 23.5 %collective-permute-start.5 = (f32[512,256]{1,0:T(8,128)S(1)}, f32[512,256]{1,0:T(8,128)S(1)}, u32[]{:S(2)}, u32[]{:S(2)}) collective-permute-start(f32[512,256]{1,0:T(8,128)S(1)} %shard_map.105.refs_3_), channel_id=1, source_target_pairs={{8,14},{13,15},{24,30},{29,31},{40,46},{45,47},{56,62},{61,63},{72... | collective-permute-start | bytes 1572872 | tf_op jit(solution)/shard_map/ppermute | solution.py:631
  31.2 11.9 %collective-permute-start = (f32[288,128]{1,0:T(8,128)S(1)}, f32[288,128]{1,0:T(8,128)S(1)}, u32[]{:S(2)}, u32[]{:S(2)}) collective-permute-start(f32[288,128]{1,0:T(8,128)S(1)} %get-tuple-element.21), channel_id=1, source_target_pairs={{0,1},{1,0},{2,3},{3,2},{4,5},{5,4},{6,7},{7,6},{8,9},{9,8},{10,11... | collective-permute-start | bytes 442376 | tf_op jit(solution)/shard_map/ppermute | solution.py:568
  31.3 11.8 %collective-permute-start.1 = (f32[288,128]{1,0:T(8,128)S(1)}, f32[288,128]{1,0:T(8,128)S(1)}, u32[]{:S(2)}, u32[]{:S(2)}) collective-permute-start(f32[288,128]{1,0:T(8,128)S(1)} %get-tuple-element.22), channel_id=1, source_target_pairs={{1,2},{2,1},{3,4},{4,3},{5,6},{6,5},{7,8},{8,7},{9,10},{10,9},{11,... | collective-permute-start | bytes 442376 | tf_op jit(solution)/shard_map/ppermute | solution.py:569
  33.2 9.8 %collective-permute-start.6 = (f32[64,128]{1,0:T(8,128)S(1)}, f32[64,128]{1,0:T(8,128)S(1)}, u32[]{:S(2)}, u32[]{:S(2)}) collective-permute-start(f32[64,128]{1,0:T(8,128)S(1)} %get-tuple-element.27), channel_id=1, source_target_pairs={{0,16},{16,32},{32,48},{48,64},{64,80},{80,96},{96,112},{112,0},{1... | collective-permute-start | bytes 98312 | tf_op jit(solution)/shard_map/ppermute | solution.py:566
  34.7 8.3 %collective-permute-start.7 = (f32[64,128]{1,0:T(8,128)S(1)}, f32[64,128]{1,0:T(8,128)S(1)}, u32[]{:S(2)}, u32[]{:S(2)}) collective-permute-start(f32[64,128]{1,0:T(8,128)S(1)} %get-tuple-element.28), channel_id=1, source_target_pairs={{16,0},{32,16},{48,32},{64,48},{80,64},{96,80},{112,96},{0,112},{1... | collective-permute-start | bytes 98312 | tf_op jit(solution)/shard_map/ppermute | solution.py:567
  53.3 14.3 %copy-start.1 = (f32[8,64,256]{2,1,0:T(8,128)S(1)}, f32[8,64,256]{2,1,0:T(8,128)}, u32[]{:S(2)}) copy-start(f32[8,64,256]{2,1,0:T(8,128)} %east_ref.3) | copy-start | bytes 1572868
  53.3 14.3 %copy-start.3 = (f32[8,64,256]{2,1,0:T(8,128)S(1)}, f32[8,64,256]{2,1,0:T(8,128)}, u32[]{:S(2)}) copy-start(f32[8,64,256]{2,1,0:T(8,128)} %north_ref.3) | copy-start | bytes 1572868
  53.4 14.3 %copy-start.8 = (s32[64,256]{1,0:T(8,128)S(1)}, s32[64,256]{1,0:T(8,128)}, u32[]{:S(2)}) copy-start(s32[64,256]{1,0:T(8,128)} %count_ref.3) | copy-start | bytes 196612
  54.7 7.6 %collective-permute-start.8 = (f32[64,128]{1,0:T(8,128)S(1)}, f32[64,128]{1,0:T(8,128)S(1)}, u32[]{:S(2)}, u32[]{:S(2)}) collective-permute-start(f32[64,128]{1,0:T(8,128)S(1)} %get-tuple-element.32), channel_id=1, source_target_pairs={{0,16},{16,32},{32,48},{48,64},{64,80},{80,96},{96,112},{112,0},{1... | collective-permute-start | bytes 98312 | tf_op jit(solution)/shard_map/ppermute | solution.py:566
  54.7 7.6 %collective-permute-start.9 = (f32[64,128]{1,0:T(8,128)S(1)}, f32[64,128]{1,0:T(8,128)S(1)}, u32[]{:S(2)}, u32[]{:S(2)}) collective-permute-start(f32[64,128]{1,0:T(8,128)S(1)} %get-tuple-element.33), channel_id=1, source_target_pairs={{16,0},{32,16},{48,32},{64,48},{80,64},{96,80},{112,96},{0,112},{1... | collective-permute-start | bytes 98312 | tf_op jit(solution)/shard_map/ppermute | solution.py:567
  60.3 1.9 %collective-permute-start.10 = (f32[64,128]{1,0:T(8,128)S(1)}, f32[64,128]{1,0:T(8,128)S(1)}, u32[]{:S(2)}, u32[]{:S(2)}) collective-permute-start(f32[64,128]{1,0:T(8,128)S(1)} %get-tuple-element.34), channel_id=1, source_target_pairs={{0,1},{1,0},{2,3},{3,2},{4,5},{5,4},{6,7},{7,6},{8,9},{9,8},{10,11... | collective-permute-start | bytes 98312 | tf_op jit(solution)/shard_map/ppermute | solution.py:568
  60.3 7.3 %collective-permute-start.11 = (f32[64,128]{1,0:T(8,128)S(1)}, f32[64,128]{1,0:T(8,128)S(1)}, u32[]{:S(2)}, u32[]{:S(2)}) collective-permute-start(f32[64,128]{1,0:T(8,128)S(1)} %get-tuple-element.35), channel_id=1, source_target_pairs={{1,2},{2,1},{3,4},{4,3},{5,6},{6,5},{7,8},{8,7},{9,10},{10,9},{11,... | collective-permute-start | bytes 98312 | tf_op jit(solution)/shard_map/ppermute | solution.py:569
where the time goes:
time: 71.5 us; the launch traced here: 70.9 us
  starting transfers between devices  25.7 us (36%)
  Pallas kernels  23.8 us (33%)
  waiting for transfers between devices  12.7 us (18%)
  local copies, waits for them, and re-layouts  7.85 us (11%)
  between operations  0.83 us (1%)
    pallas_call x6, Pallas kernels, call(): pl.pallas_call(kernel, out_shape=[jax.ShapeDtypeStruct(shape, F32) for sh...  23.8 us
    ppermute x2, starting transfers between devices, exchange(): lax.ppermute(to_west, 'gx', WESTWARD)  12 us
    unnamed x26, local copies, waits for them, and re-layouts  7.85 us
    ppermute x3, starting transfers between devices, local(): lax.ppermute(part, 'gy', list(pairs))  6.95 us
    ppermute x2, waiting for transfers between devices, exchange(): lax.ppermute(other, ('gx', 'gy'), OTHERS)  5.39 us
    ppermute x3, waiting for transfers between devices, local(): lax.ppermute(part, 'gy', list(pairs))  5.31 us
    ppermute x2, starting transfers between devices, exchange(): lax.ppermute(other, ('gx', 'gy'), OTHERS)  3.83 us
    ppermute x2, waiting for transfers between devices, exchange(): lax.ppermute(to_east, 'gx', EASTWARD)  1.96 us
  transfers between devices with their start and end apart: 12, of which 4 were waited for; matrix products, arithmetic and copies ran while one was open for 0% of the time, Pallas kernels for 14%

commit v1 on v0

--- a/solution.py
+++ b/solution.py
@@ -18,21 +18,25 @@
 GY = 16
 SLOT_ROWS = 32
 ATMOS_ROWS = 16
-HELPERS = ((8, GY - 2), (13, GY - 1))
+HELPED_BY = {8: GY - 2, 12: GY - 1}
+DENSE = ((8, GY - 2), (12, GY - 1))
 ENTRY_STEPS = (
-    ((9, 8), (10, 13), (7, 14), (8, 15)),
-    ((10, 8), (11, 13), (12, 14), (7, 15)),
-    ((11, 8), (12, 13), (9, 15)),
+    ((10, GY - 2), (7, GY - 1)),
+    ((11, GY - 2), (8, GY - 1)),
+    ((12, GY - 2), (9, GY - 1)),
+    ((10, GY - 1),),
 )
-HELPED_BY = {helper: target for helper, target in HELPERS}
 CHANNELS = TRACERS * NZ
 COUNT_AT = 24
 RIM = 32
-PAYLOAD = 3 * SLOT_ROWS + FIELDS * ATMOS_ROWS
+LIST = 3 * SLOT_ROWS
+ATMOS = FIELDS * ATMOS_ROWS
+PAYLOAD = LIST + ATMOS
 CHUNK_ROWS = 16
 CHUNK = CHUNK_ROWS * LANES
 CHUNKS = SLOT_ROWS // CHUNK_ROWS
 VMEM_LIMIT = 48 * 1024 * 1024
+PACK_LIMIT = 63 * 1024 * 1024
 F32 = jnp.float32
 BF16 = jnp.bfloat16
 F8 = jnp.float8_e4m3fn
@@ -40,14 +44,14 @@
 
 
 def call(kernel, out_shapes, operands, scratch=(), flops=0, moved=4_000_000, in_hbm=False):
-    place = pl.ANY if in_hbm else pltpu.VMEM
+    place = pltpu.HBM if in_hbm else pltpu.VMEM
     return pl.pallas_call(
         kernel,
         out_shape=[jax.ShapeDtypeStruct(shape, F32) for shape in out_shapes],
         in_specs=[pl.BlockSpec(memory_space=place) for _ in operands],
         out_specs=[pl.BlockSpec(memory_space=pltpu.VMEM) for _ in out_shapes],
         scratch_shapes=list(scratch),
-        compiler_params=pltpu.CompilerParams(vmem_limit_bytes=VMEM_LIMIT),
+        compiler_params=pltpu.CompilerParams(vmem_limit_bytes=PACK_LIMIT if in_hbm else VMEM_LIMIT),
         cost_estimate=pl.CostEstimate(flops=flops, bytes_accessed=moved, transcendentals=0),
     )(*operands)
 
@@ -90,77 +94,61 @@
     return default
 
 
-def pack_kernel(
-    tracers_hbm,
-    east_hbm,
-    north_hbm,
-    count_hbm,
-    atmos_hbm,
-    source_hbm,
-    target_hbm,
-    weight_hbm,
-    to_east_ref,
-    to_west_ref,
-    sibling_ref,
-    other_ref,
-    first_ref,
-    second_ref,
-    *refs,
-):
-    entry_refs, scratch = refs[: len(ENTRY_STEPS)], refs[len(ENTRY_STEPS) :]
-    tracers_ref, east_ref, north_ref, count_ref, atmos_ref, source_ref, target_ref, weight_ref = scratch[:8]
-    sems = scratch[8]
-    here = lax.axis_index("gy")
-    even = is_even()
-    lists = ((source_hbm, source_ref), (target_hbm, target_ref), (weight_hbm, weight_ref))
+def among(here, table):
+    return functools.reduce(jnp.logical_or, [here == key for key in table])
+
+
+def list_into(lists, out_ref, at, tile, valid=None):
+    rows = pl.ds(pl.multiple_of(tile * SLOT_ROWS, SLOT_ROWS), SLOT_ROWS)
+    for kind, ref in enumerate(lists):
+        part = ref[rows, :].astype(F32)
+        if kind == 2 and valid is not None:
+            part = jnp.where(valid, part, 0.0)
+        out_ref[at + kind * SLOT_ROWS : at + (kind + 1) * SLOT_ROWS, :] = part
+
+
+def pack_kernel(*refs):
+    steps = len(ENTRY_STEPS)
+    froms, refs = refs[:8], refs[8:]
+    (to_east_ref, to_west_ref, sibling_ref, other_ref), refs = refs[:4], refs[4:]
+    entry_refs, intos, (cells_ref, sems) = refs[:steps], refs[steps:-2], refs[-2:]
+    tracers_ref, east_ref, north_ref, count_ref, source_ref, target_ref, weight_ref, atmos_ref = intos
     copies = [
-        *lists,
-        (atmos_hbm, atmos_ref),
-        (tracers_hbm, tracers_ref),
-        (east_hbm.at[:, :, pl.ds(LANES, LANES)], east_ref),
-        (north_hbm.at[:, pl.ds(ROWS - 8, 8), :], north_ref),
-        (count_hbm, count_ref),
-    ]
-    copies = [
-        pltpu.make_async_copy(source, into, sems.at[n]) for n, (source, into) in enumerate(copies)
+        pltpu.make_async_copy(array, into, sems.at[n])
+        for n, (array, into) in enumerate(zip(froms, intos, strict=True))
     ]
     for copy in copies:
         copy.start()
-    for copy in copies[:4]:
+    for copy in copies:
         copy.wait()
-
-    def slot_into(out_ref, at, tile, valid=None):
-        rows = pl.ds(pl.multiple_of(tile * SLOT_ROWS, SLOT_ROWS), SLOT_ROWS)
-        out_ref[at : at + SLOT_ROWS, :] = source_ref[rows, :].astype(F32)
-        out_ref[at + SLOT_ROWS : at + 2 * SLOT_ROWS, :] = target_ref[rows, :].astype(F32)
-        weight = weight_ref[rows, :]
-        if valid is not None:
-            weight = jnp.where(valid, weight, 0.0)
-        out_ref[at + 2 * SLOT_ROWS : at + 3 * SLOT_ROWS, :] = weight
-        for field in range(FIELDS):
-            for row in range(ATMOS_ROWS):
-                to = at + 3 * SLOT_ROWS + row * FIELDS + field
-                out_ref[to : to + 1, :] = atmos_ref[field, row : row + 1, :]
-
+    here = lax.axis_index("gy")
+    even = is_even()
+    lists = (source_ref, target_ref, weight_ref)
+    for field in range(FIELDS):
+        for row in range(ATMOS_ROWS):
+            to = row * FIELDS + field
+            cells_ref[to : to + 1, :] = atmos_ref[field, row : row + 1, :]
+    cells = cells_ref[...]
     for pairs, out_ref in zip(ENTRY_STEPS, entry_refs, strict=True):
-        table = {source: HELPED_BY.get(target, target) for source, target in pairs}
-        slot_into(out_ref, 0, chosen(here, table, here))
-    slot_into(first_ref, 0, chosen(here, HELPED_BY, here))
-    helps = functools.reduce(jnp.logical_or, [here == helper for helper in HELPED_BY])
-    slot_into(second_ref, 0, here, helps)
-    slot_into(sibling_ref, 2 * RIM, jnp.where(even, here + 1, here - 1))
+        list_into(lists, out_ref, 0, chosen(here, dict(pairs), here))
+        out_ref[LIST:PAYLOAD, :] = cells
+    partner = here ^ 1
+    list_into(lists, sibling_ref, 2 * RIM, chosen(partner, HELPED_BY, partner))
+    list_into(lists, sibling_ref, 2 * RIM + LIST, partner, among(partner, HELPED_BY))
+    sibling_ref[2 * RIM + 2 * LIST :, :] = cells
     away = jnp.clip(jnp.where(even, here - 1, here + 1), 0, GY - 1)
-    slot_into(other_ref, 2 * RIM, away, here != GY - 1)
-
-    for copy in copies[4:]:
-        copy.wait()
+    below_top = here != GY - 1
+    helped = jnp.logical_and(below_top, among(away, HELPED_BY))
+    list_into(lists, other_ref, 2 * RIM, chosen(away, HELPED_BY, away), helped)
+    list_into(lists, other_ref, 2 * RIM + LIST, away, below_top)
+    other_ref[2 * RIM + 2 * LIST :, :] = cells
 
     def east_column(channel, row):
         rows = pl.ds(row, 8)
         if channel < CHANNELS:
             return tracers_ref[channel, rows, LANES:], LANES - 1
         if channel < COUNT_AT:
-            return east_ref[channel - CHANNELS, rows, :], LANES - 1
+            return east_ref[channel - CHANNELS, rows, LANES:], LANES - 1
         return count_ref[rows, LANES:].astype(F32), LANES - 1
 
     def west_column(channel, row):
@@ -176,7 +164,7 @@
         if channel < CHANNELS:
             return tracers_ref[channel, ROWS - 1 : ROWS, :]
         if channel < COUNT_AT:
-            return north_ref[channel - CHANNELS, 7:8, :]
+            return north_ref[channel - CHANNELS, ROWS - 1 : ROWS, :]
         return count_ref[ROWS - 1 : ROWS, :].astype(F32)
 
     def bottom_of(channel):
@@ -207,10 +195,10 @@
     *more_refs,
 ):
     if forced:
-        out_ref, gain_ref = more_refs[:2]
+        out_ref, gain_ref = more_refs[-6:-4]
     else:
         forcing_ref, out_ref = more_refs[:2]
-    from_south_ref, top_ref, static_south_ref, static_top_ref = more_refs[2:]
+    from_south_ref, top_ref, static_south_ref, static_top_ref = more_refs[-4:]
     even = is_even()
     on_top = lax.axis_index("gy") == GY - 1
     lane = lax.broadcasted_iota(jnp.int32, (8, LANES), 1)
@@ -405,33 +393,51 @@
     lax.fori_loop(0, ROWS // 8, block_step, 0)
 
 
-def land_kernel(offsets, continued, *refs):
-    slot_refs, refs = refs[: len(offsets)], refs[len(offsets) :]
-    if continued:
-        start_ref, refs = refs[0], refs[1:]
+def land_kernel(slots, own_slot, reset, *refs):
+    operand_refs, refs = refs[:-8], refs[-8:]
+    if own_slot:
+        own, operand_refs = operand_refs[:4], operand_refs[4:]
+    here = lax.axis_index("gy")
+    helps = among(here, HELPED_BY)
+    if reset is not None:
+        start_ref = operand_refs[-1]
     total_ref, lists_ref, cells_ref, high_ref, low_ref, high_hot_ref, low_hot_ref, live_ref = refs
     largest = jnp.zeros((8, LANES), F32)
-    for slot, (ref, at) in enumerate(zip(slot_refs, offsets, strict=True)):
+    if own_slot:
+        tile = here if reset else chosen(here, HELPED_BY, here)
+        rows = pl.ds(pl.multiple_of(tile * SLOT_ROWS, SLOT_ROWS), SLOT_ROWS)
         for kind in range(3):
-            rows = pl.ds(at + kind * SLOT_ROWS, SLOT_ROWS)
+            part = own[kind][rows, :].astype(F32)
+            if kind == 2 and reset:
+                part = jnp.where(helps, part, 0.0)
+            lists_ref[kind, 0:SLOT_ROWS, :] = part
+        for field in range(FIELDS):
+            largest = jnp.maximum(largest, jnp.abs(own[3][field, 0:8, :]))
+            largest = jnp.maximum(largest, jnp.abs(own[3][field, 8:16, :]))
+            for row in range(ATMOS_ROWS):
+                cells_ref[0, row, field : field + 1, :] = own[3][field, row : row + 1, :]
+    count = own_slot + len(slots)
+    for slot, (operand, list_at, cells_at) in enumerate(slots, own_slot):
+        ref = operand_refs[operand]
+        for kind in range(3):
+            rows = pl.ds(list_at + kind * SLOT_ROWS, SLOT_ROWS)
             lists_ref[kind, pl.ds(slot * SLOT_ROWS, SLOT_ROWS), :] = ref[rows, :]
         for row in range(ATMOS_ROWS):
-            cells = ref[pl.ds(at + 3 * SLOT_ROWS + row * FIELDS, FIELDS), :]
+            cells = ref[pl.ds(cells_at + row * FIELDS, FIELDS), :]
             cells_ref[slot, row] = cells
             largest = jnp.maximum(largest, jnp.abs(cells))
     scale = LOW_TOP / jnp.maximum(jnp.max(largest), 1e-30)
     unscale = 1.0 / scale
 
     found = jnp.int32(0)
-    for index in range(len(offsets) * CHUNKS):
+    for index in range(count * CHUNKS):
         weights = lists_ref[2, pl.ds(index * CHUNK_ROWS, CHUNK_ROWS), :]
         live_ref[found] = index
         found = found + (jnp.max(weights) > 0.0).astype(jnp.int32)
 
-    if continued:
-        helps = functools.reduce(
-            jnp.logical_or, [lax.axis_index("gy") == helper for helper in HELPED_BY]
-        )
+    if reset is None:
+        total_ref[...] = jnp.zeros_like(total_ref)
+    elif reset:
 
         @pl.when(helps)
         def _():
@@ -441,13 +447,13 @@
         def _():
             total_ref[...] = start_ref[...]
     else:
-        total_ref[...] = jnp.zeros_like(total_ref)
+        total_ref[...] = start_ref[...]
     ones, zeros = jnp.ones((), BF16), jnp.zeros((), BF16)
     iota = lax.broadcasted_iota(jnp.int32, (COLUMNS, LANES), 0).astype(F32).astype(BF16)
 
-    def hot(values, entry, count):
+    def hot(values, entry, height):
         line = jnp.broadcast_to(values[entry : entry + 1, :], (16, LANES)).astype(BF16)
-        return [jnp.where(line == iota[at : at + 16], ones, zeros) for at in range(0, count, 16)]
+        return [jnp.where(line == iota[at : at + 16], ones, zeros) for at in range(0, height, 16)]
 
     def chunk_step(at, carry):
         index = live_ref[at]
@@ -570,12 +576,12 @@
     )
 
 
-def land(slots, offsets, start=()):
-    count = len(slots)
+def land(operands, slots, own_slot, reset):
+    count = own_slot + len(slots)
     (total,) = call(
-        functools.partial(land_kernel, offsets, bool(start)),
+        functools.partial(land_kernel, slots, own_slot, reset),
         [(FIELDS * ROWS, COLUMNS)],
-        [*slots, *start],
+        operands,
         [
             pltpu.VMEM((3, count * SLOT_ROWS, LANES), F32),
             pltpu.VMEM((count, ATMOS_ROWS, FIELDS, LANES), F32),
@@ -585,8 +591,7 @@
             pltpu.VMEM((COLUMNS, CHUNK), F8),
             pltpu.SMEM((count * CHUNKS + 1,), jnp.int32),
         ],
-        flops=4_000_000_000,
-        moved=20_000_000,
+        moved=100_000,
     )
     return total
 
@@ -603,39 +608,44 @@
     intersection_weight,
 ):
     q = tracers.reshape(CHANNELS, ROWS, COLUMNS)
-    lists = [intersection_source, intersection_target, intersection_weight]
+    statics = [east_speed, north_speed, level_count, vertical_mix]
+    lists = [intersection_source, intersection_target, intersection_weight, atmosphere_flux]
     column_rim, row_rim = (ROWS, LANES), (2 * RIM, LANES)
-    near, slot = (2 * RIM + PAYLOAD, LANES), (PAYLOAD, LANES)
+    both = (2 * RIM + LIST + PAYLOAD, LANES)
     steps = len(ENTRY_STEPS)
-    to_east, to_west, sibling, other, first, second, *entries = call(
+    packed = call(
         pack_kernel,
-        [column_rim, column_rim, near, near] + [slot] * (2 + steps),
-        [q, east_speed, north_speed, level_count, atmosphere_flux, *lists],
+        [column_rim, column_rim, both, both] + [(PAYLOAD, LANES)] * steps,
+        [q, *statics[:3], *lists],
         [
-            pltpu.VMEM(q.shape, F32),
-            pltpu.VMEM((NZ, ROWS, LANES), F32),
-            pltpu.VMEM((NZ, 8, COLUMNS), F32),
-            pltpu.VMEM(level_count.shape, jnp.int32),
-            pltpu.VMEM(atmosphere_flux.shape, F32),
-            *[pltpu.VMEM(part.shape, part.dtype) for part in lists],
+            *[pltpu.VMEM(part.shape, part.dtype) for part in (q, *statics[:3], *lists)],
+            pltpu.VMEM((ATMOS, LANES), F32),
             pltpu.SemaphoreType.DMA((8,)),
         ],
         in_hbm=True,
     )
     entries = [
         lax.ppermute(part, "gy", list(pairs))
-        for part, pairs in zip(entries, ENTRY_STEPS, strict=True)
+        for part, pairs in zip(packed[4:], ENTRY_STEPS, strict=True)
     ]
-    rims = exchange(to_east, to_west, sibling, other)
-    partial = land([first, *entries], (0,) * (1 + steps))
-    helped = lax.ppermute(partial, "gy", list(HELPERS))
-    total = land([second, rims[2], rims[3]], (0, 2 * RIM, 2 * RIM), (partial,))
-    statics = [east_speed, north_speed, level_count, vertical_mix]
+    own = land(lists, (), 1, None)
+    rims = exchange(*packed[:4])
+    first, second, cells = 2 * RIM, 2 * RIM + LIST, 2 * RIM + 2 * LIST
+    most = land([rims[2], own], ((0, first, cells),), 0, False)
+    partial = land([rims[3], *entries, most], ((0, first, cells),), 0, False)
+    helped = lax.ppermute(partial, "gy", list(DENSE))
+    total = land(
+        [*lists, rims[2], rims[3], *entries, partial],
+        ((0, second, cells), (1, second, cells))
+        + tuple((2 + step, 0, LIST) for step in range(steps)),
+        1,
+        True,
+    )
     rim_scratch = [pltpu.VMEM(row_rim, F32)] * 4
     solved, gain = call(
         functools.partial(step_kernel, True),
         [q.shape, east_speed.shape],
-        [q, *rims, *rims, *statics],
+        [q, *rims, *rims, *statics, partial],
         rim_scratch,
         moved=8_000_000,
     )

time: 71.5 us -> 59.4 us (0.83)
  the two profiles are of different devices: /device:TPU:32 before, /device:TPU:57 now
where the time goes in v1:
time: 59.4 us; the launch traced here: 58.7 us
  starting transfers between devices  26.2 us (44%)
  Pallas kernels  24.2 us (41%)
  waiting for transfers between devices  7.27 us (12%)
  between operations  1 us (2%)
    pallas_call x8, Pallas kernels, call(): pl.pallas_call(kernel, out_shape=[jax.ShapeDtypeStruct(shape, F32) for sh...  24.2 us
    ppermute x2, starting transfers between devices, exchange(): lax.ppermute(to_west, 'gx', WESTWARD)  10.2 us
    ppermute x2, starting transfers between devices, exchange(): lax.ppermute(other, ('gx', 'gy'), OTHERS)  8.7 us
    ppermute x2, waiting for transfers between devices, exchange(): lax.ppermute(other, ('gx', 'gy'), OTHERS)  6.41 us
    ppermute x4, starting transfers between devices, local(): lax.ppermute(part, 'gy', list(pairs))  5.17 us
    ppermute x1, starting transfers between devices, local(): helped = lax.ppermute(partial, 'gy', list(DENSE))  1.29 us
  transfers between devices with their start and end apart: 13, of which 2 were waited for; matrix products, arithmetic and copies ran while one was open for 0% of the time, Pallas kernels for 27%

profile of v1, /device:TPU:57, one launch (start us, length us, event | category | flops | bytes accessed | tf_op | source)
XLA Modules:
  0.0 58.7 jit_solution(11979299076332958252)
XLA Ops:
  0.6 0.0 copy-start.3
  0.6 0.0 copy-start.4
  0.7 0.0 copy-start.5
  0.7 0.0 copy-start.8
  0.7 3.2 %shard_map.104 = (f32[64,128]{1,0:T(8,128)}, f32[64,128]{1,0:T(8,128)}, f32[384,128]{1,0:T(8,128)}, f32[384,128]{1,0:T(8,128)}, f32[224,128]{1,0:T(8,128)}, /*in...) custom-call(f32[16,64,256]{2,1,0:T(8,128)} %bitcast.2, f32[8,64,256]{2,1,0:T(8,128)} %east_ref.3, ...), custom_call_target="tpu_custom_call" | custom-call | bytes 4000000 | tf_op jit(solution)/shard_map/pallas_call | solution.py:48
  3.9 0.8 %collective-permute-start = (f32[384,128]{1,0:T(8,128)}, f32[384,128]{1,0:T(8,128)S(1)}, u32[]{:S(2)}, u32[]{:S(2)}) collective-permute-start(f32[384,128]{1,0:T(8,128)} %get-tuple-element.19), channel_id=1, source_target_pairs={{0,1},{1,0},{2,3},{3,2},{4,5},{5,4},{6,7},{7,6},{8,9},{9,8},{10,11... | collective-permute-start | bytes 589832 | tf_op jit(solution)/shard_map/ppermute | solution.py:574
  4.7 6.8 %collective-permute-start.1 = (f32[384,128]{1,0:T(8,128)}, f32[384,128]{1,0:T(8,128)S(1)}, u32[]{:S(2)}, u32[]{:S(2)}) collective-permute-start(f32[384,128]{1,0:T(8,128)} %get-tuple-element.20), channel_id=1, source_target_pairs={{1,2},{2,1},{3,4},{4,3},{5,6},{6,5},{7,8},{8,7},{9,10},{10,9},{11,... | collective-permute-start | bytes 589832 | tf_op jit(solution)/shard_map/ppermute | solution.py:575
  11.5 1.3 %collective-permute-start.2 = (f32[224,128]{1,0:T(8,128)}, f32[224,128]{1,0:T(8,128)S(1)}, u32[]{:S(2)}, u32[]{:S(2)}) collective-permute-start(f32[224,128]{1,0:T(8,128)} %get-tuple-element.21), channel_id=1, source_target_pairs={{10,14},{7,15},{26,30},{23,31},{42,46},{39,47},{58,62},{55,63},{74... | collective-permute-start | bytes 344072 | tf_op jit(solution)/shard_map/ppermute | solution.py:628
  12.8 1.3 %collective-permute-start.3 = (f32[224,128]{1,0:T(8,128)}, f32[224,128]{1,0:T(8,128)S(1)}, u32[]{:S(2)}, u32[]{:S(2)}) collective-permute-start(f32[224,128]{1,0:T(8,128)} %get-tuple-element.22), channel_id=1, source_target_pairs={{11,14},{8,15},{27,30},{24,31},{43,46},{40,47},{59,62},{56,63},{75... | collective-permute-start | bytes 344072 | tf_op jit(solution)/shard_map/ppermute | solution.py:628
  14.1 1.3 %collective-permute-start.4 = (f32[224,128]{1,0:T(8,128)}, f32[224,128]{1,0:T(8,128)S(1)}, u32[]{:S(2)}, u32[]{:S(2)}) collective-permute-start(f32[224,128]{1,0:T(8,128)} %get-tuple-element.23), channel_id=1, source_target_pairs={{12,14},{9,15},{28,30},{25,31},{44,46},{41,47},{60,62},{57,63},{76... | collective-permute-start | bytes 344072 | tf_op jit(solution)/shard_map/ppermute | solution.py:628
  15.4 0.0 collective-permute-done.refs_0_.refs_4_.from_sibling_ref.static_sibling_ref
  15.4 1.3 %collective-permute-start.5 = (f32[224,128]{1,0:T(8,128)}, f32[224,128]{1,0:T(8,128)S(1)}, u32[]{:S(2)}, u32[]{:S(2)}) collective-permute-start(f32[224,128]{1,0:T(8,128)} %get-tuple-element.24), channel_id=1, source_target_pairs={{10,15},{26,31},{42,47},{58,63},{74,79},{90,95},{106,111},{122,127}} | collective-permute-start | bytes 344072 | tf_op jit(solution)/shard_map/ppermute | solution.py:628
  16.7 0.0 copy-done.3
  16.7 0.0 copy-done.4
  16.7 0.0 copy-done.5
  16.7 0.0 copy-done.8
  16.7 2.8 %shard_map.105.refs_1_ = f32[512,256]{1,0:T(8,128)S(1)} custom-call(s32[512,128]{1,0:T(8,128)S(1)} %copy-done.3, s32[512,128]{1,0:T(8,128)S(1)} %copy-done.4, f32[512,128]{1,0:T(8,128)S(1)} %copy-done.5, f32[8,16,128]{2,1,0:T(8,128)S(1)} %copy-done.8), custom_call_target="tpu_custom_call" | custom-call | bytes 100000 | tf_op jit(solution)/shard_map/pallas_call | solution.py:48
  19.5 2.8 %shard_map.106.refs_5_ = f32[512,256]{1,0:T(8,128)S(1)} custom-call(f32[384,128]{1,0:T(8,128)S(1)} %collective-permute-done.refs_0_.refs_4_.from_sibling_ref.static_sibling_ref, f32[512,256]{1,0:T(8,128)S(1)} %shard_map.105.refs_1_), custom_call_target="tpu_custom_call" | custom-call | bytes 100000 | tf_op jit(solution)/shard_map/pallas_call | solution.py:48
  22.3 0.0 copy-start.10
  22.3 0.0 collective-permute-done.2.refs_1_.refs_6_
  22.3 0.0 collective-permute-done.3.refs_2_.refs_7_
  22.4 0.0 collective-permute-done.4.refs_3_.refs_8_
  22.4 0.8 %collective-permute-done.5.refs_4_.refs_9_ = f32[224,128]{1,0:T(8,128)S(1)} collective-permute-done((f32[224,128]{1,0:T(8,128)}, f32[224,128]{1,0:T(8,128)S(1)}, u32[]{:S(2)}, u32[]{:S(2)}) %collective-permute-start.5) | collective-permute-done | bytes 114720 | tf_op jit(solution)/shard_map/ppermute | solution.py:628
  23.2 0.0 collective-permute-done.1.refs_0_.refs_5_.from_other_ref.static_other_ref
  23.2 0.2 shard_map.107.refs_10_.more_refs_0_
  23.4 1.3 %collective-permute-start.6 = (f32[512,256]{1,0:T(8,128)S(1)}, f32[512,256]{1,0:T(8,128)S(1)}, u32[]{:S(2)}, u32[]{:S(2)}) collective-permute-start(f32[512,256]{1,0:T(8,128)S(1)} %shard_map.107.refs_10_.more_refs_0_), channel_id=1, source_target_pairs={{8,14},{12,15},{24,30},{28,31},{40,46},{44,47},{56,62},{60,63},{72... | collective-permute-start | bytes 1572872 | tf_op jit(solution)/shard_map/ppermute | solution.py:636
  24.7 0.1 collective-permute-start.7
  24.8 0.0 copy-start
  24.8 0.0 copy-start.1
  24.9 0.0 copy-start.2
  24.9 0.0 copy-start.6
  24.9 0.0 copy-start.7
  24.9 5.1 %collective-permute-start.8 = (f32[64,128]{1,0:T(8,128)S(1)}, f32[64,128]{1,0:T(8,128)S(1)}, u32[]{:S(2)}, u32[]{:S(2)}) collective-permute-start(f32[64,128]{1,0:T(8,128)S(1)} %copy-done.9), channel_id=1, source_target_pairs={{16,0},{32,16},{48,32},{64,48},{80,64},{96,80},{112,96},{0,112},{1... | collective-permute-start | bytes 98312 | tf_op jit(solution)/shard_map/ppermute | solution.py:573
  30.0 8.1 %shard_map.108.total_ref = f32[512,256]{1,0:T(8,128)S(1)} custom-call(s32[512,128]{1,0:T(8,128)S(1)} %copy-done.3, s32[512,128]{1,0:T(8,128)S(1)} %copy-done.4, f32[512,128]{1,0:T(8,128)S(1)} %copy-done.5, f32[8,16,128]{2,1,0:T(8,128)S(1)} %copy-done.8, f32[384,128]{1,0:T(8,128)S(1)} %collective-permute-done.refs_0_.refs_4_.from_sibling_ref.static_sibling_ref, ...), custom_call_target="tpu_custom_call" | custom-call | bytes 100000 | tf_op jit(solution)/shard_map/pallas_call | solution.py:48
  38.1 0.0 collective-permute-done.7.from_west_ref.static_west_ref
  38.1 0.0 collective-permute-done.8.from_east_ref.static_east_ref
  38.2 2.4 %shard_map.109 = (f32[16,64,256]{2,1,0:T(8,128)S(1)}, f32[8,64,256]{2,1,0:T(8,128)S(1)}) custom-call(f32[16,64,256]{2,1,0:T(8,128)S(1)} %bitcast.3, f32[64,128]{1,0:T(8,128)S(1)} %collective-permute-done.7.from_west_ref.static_west_ref, f32[64,128]{1,0:T(8,128)S(1)} %collective-permute-done.8.from_east_ref.static_east_ref, ...), custom_call_target="tpu_custom_call" | custom-call | bytes 8000000 | tf_op jit(solution)/shard_map/pallas_call | solution.py:48
  40.6 0.0 collective-permute-done.6.helped_ref
  40.6 1.3 %shard_map.110 = (f32[16,64,256]{2,1,0:T(8,128)S(1)}, f32[8,64,256]{2,1,0:T(8,128)}, f32[2,64,256]{2,1,0:T(8,128)S(1)}, f32[64,128]{1,0:T(8,128)S(1)}, f32[64,12...) custom-call(f32[512,256]{1,0:T(8,128)S(1)} %shard_map.108.total_ref, ...), custom_call_target="tpu_custom_call" | custom-call | bytes 4000000 | tf_op jit(solution)/shard_map/pallas_call | solution.py:48
  41.9 0.0 collective-permute-start.9
  41.9 5.1 %collective-permute-start.10 = (f32[64,128]{1,0:T(8,128)S(1)}, f32[64,128]{1,0:T(8,128)S(1)}, u32[]{:S(2)}, u32[]{:S(2)}) collective-permute-start(f32[64,128]{1,0:T(8,128)S(1)} %get-tuple-element.31), channel_id=1, source_target_pairs={{16,0},{32,16},{48,32},{64,48},{80,64},{96,80},{112,96},{0,112},{1... | collective-permute-start | bytes 98312 | tf_op jit(solution)/shard_map/ppermute | solution.py:573
  47.0 0.0 collective-permute-start.11
  47.0 1.9 %collective-permute-start.12 = (f32[64,128]{1,0:T(8,128)S(1)}, f32[64,128]{1,0:T(8,128)S(1)}, u32[]{:S(2)}, u32[]{:S(2)}) collective-permute-start(f32[64,128]{1,0:T(8,128)S(1)} %get-tuple-element.33), channel_id=1, source_target_pairs={{1,2},{2,1},{3,4},{4,3},{5,6},{6,5},{7,8},{8,7},{9,10},{10,9},{11,... | collective-permute-start | bytes 98312 | tf_op jit(solution)/shard_map/ppermute | solution.py:575
  48.9 0.0 collective-permute-done.9.from_west_ref
  48.9 0.0 collective-permute-done.10.from_east_ref
  48.9 0.0 collective-permute-done.11.from_sibling_ref
  49.0 6.4 %collective-permute-done.12.from_other_ref = f32[64,128]{1,0:T(8,128)S(1)} collective-permute-done((f32[64,128]{1,0:T(8,128)S(1)}, f32[64,128]{1,0:T(8,128)S(1)}, u32[]{:S(2)}, u32[]{:S(2)}) %collective-permute-start.12) | collective-permute-done | bytes 32800 | tf_op jit(solution)/shard_map/ppermute | solution.py:575
  55.4 3.3 %shard_map.111 = f32[16,64,256]{2,1,0:T(8,128)} custom-call(f32[16,64,256]{2,1,0:T(8,128)S(1)} %get-tuple-element.29.q_ref, f32[64,128]{1,0:T(8,128)S(1)} %collective-permute-done.9.from_west_ref, f32[64,128]{1,0:T(8,128)S(1)} %collective-permute-done.10.from_east_ref, f32[64,128]{1,0:T(8,128)S(1)} %collective-permute-done.11.from_sibling_ref, ...), custom_call_target="tpu_custom_call" | custom-call | bytes 8000000 | tf_op jit(solution)/shard_map/pallas_call | solution.py:48
  (8 shorter events, 0.0 us)
Async XLA Ops:
  0.6 16.0 %copy-start.3 = (s32[512,128]{1,0:T(8,128)S(1)}, s32[512,128]{1,0:T(8,128)}, u32[]{:S(2)}) copy-start(s32[512,128]{1,0:T(8,128)} %refs_0_.3) | copy-start | bytes 786436
  0.6 16.0 %copy-start.4 = (s32[512,128]{1,0:T(8,128)S(1)}, s32[512,128]{1,0:T(8,128)}, u32[]{:S(2)}) copy-start(s32[512,128]{1,0:T(8,128)} %refs_1_.5) | copy-start | bytes 786436
  0.7 16.0 %copy-start.5 = (f32[512,128]{1,0:T(8,128)S(1)}, f32[512,128]{1,0:T(8,128)}, u32[]{:S(2)}) copy-start(f32[512,128]{1,0:T(8,128)} %refs_2_.5) | copy-start | bytes 786436
  0.7 16.0 %copy-start.8 = (f32[8,16,128]{2,1,0:T(8,128)S(1)}, f32[8,16,128]{2,1,0:T(8,128)}, u32[]{:S(2)}) copy-start(f32[8,16,128]{2,1,0:T(8,128)} %refs_3_.5) | copy-start | bytes 196612
  3.9 11.5 %collective-permute-start = (f32[384,128]{1,0:T(8,128)}, f32[384,128]{1,0:T(8,128)S(1)}, u32[]{:S(2)}, u32[]{:S(2)}) collective-permute-start(f32[384,128]{1,0:T(8,128)} %get-tuple-element.19), channel_id=1, source_target_pairs={{0,1},{1,0},{2,3},{3,2},{4,5},{5,4},{6,7},{7,6},{8,9},{9,8},{10,11... | collective-permute-start | bytes 589832 | tf_op jit(solution)/shard_map/ppermute | solution.py:574
  4.7 18.5 %collective-permute-start.1 = (f32[384,128]{1,0:T(8,128)}, f32[384,128]{1,0:T(8,128)S(1)}, u32[]{:S(2)}, u32[]{:S(2)}) collective-permute-start(f32[384,128]{1,0:T(8,128)} %get-tuple-element.20), channel_id=1, source_target_pairs={{1,2},{2,1},{3,4},{4,3},{5,6},{6,5},{7,8},{8,7},{9,10},{10,9},{11,... | collective-permute-start | bytes 589832 | tf_op jit(solution)/shard_map/ppermute | solution.py:575
  11.5 10.9 %collective-permute-start.2 = (f32[224,128]{1,0:T(8,128)}, f32[224,128]{1,0:T(8,128)S(1)}, u32[]{:S(2)}, u32[]{:S(2)}) collective-permute-start(f32[224,128]{1,0:T(8,128)} %get-tuple-element.21), channel_id=1, source_target_pairs={{10,14},{7,15},{26,30},{23,31},{42,46},{39,47},{58,62},{55,63},{74... | collective-permute-start | bytes 344072 | tf_op jit(solution)/shard_map/ppermute | solution.py:628
  12.8 9.6 %collective-permute-start.3 = (f32[224,128]{1,0:T(8,128)}, f32[224,128]{1,0:T(8,128)S(1)}, u32[]{:S(2)}, u32[]{:S(2)}) collective-permute-start(f32[224,128]{1,0:T(8,128)} %get-tuple-element.22), channel_id=1, source_target_pairs={{11,14},{8,15},{27,30},{24,31},{43,46},{40,47},{59,62},{56,63},{75... | collective-permute-start | bytes 344072 | tf_op jit(solution)/shard_map/ppermute | solution.py:628
  14.1 8.3 %collective-permute-start.4 = (f32[224,128]{1,0:T(8,128)}, f32[224,128]{1,0:T(8,128)S(1)}, u32[]{:S(2)}, u32[]{:S(2)}) collective-permute-start(f32[224,128]{1,0:T(8,128)} %get-tuple-element.23), channel_id=1, source_target_pairs={{12,14},{9,15},{28,30},{25,31},{44,46},{41,47},{60,62},{57,63},{76... | collective-permute-start | bytes 344072 | tf_op jit(solution)/shard_map/ppermute | solution.py:628
  15.4 7.8 %collective-permute-start.5 = (f32[224,128]{1,0:T(8,128)}, f32[224,128]{1,0:T(8,128)S(1)}, u32[]{:S(2)}, u32[]{:S(2)}) collective-permute-start(f32[224,128]{1,0:T(8,128)} %get-tuple-element.24), channel_id=1, source_target_pairs={{10,15},{26,31},{42,47},{58,63},{74,79},{90,95},{106,111},{122,127}} | collective-permute-start | bytes 344072 | tf_op jit(solution)/shard_map/ppermute | solution.py:628
  22.3 2.4 %copy-start.10 = (f32[64,128]{1,0:T(8,128)S(1)}, f32[64,128]{1,0:T(8,128)}, u32[]{:S(2)}) copy-start(f32[64,128]{1,0:T(8,128)} %get-tuple-element.25) | copy-start | bytes 98308
  22.3 2.5 %copy-start.9 = (f32[64,128]{1,0:T(8,128)S(1)}, f32[64,128]{1,0:T(8,128)}, u32[]{:S(2)}) copy-start(f32[64,128]{1,0:T(8,128)} %get-tuple-element.26) | copy-start | bytes 98308
  23.4 17.2 %collective-permute-start.6 = (f32[512,256]{1,0:T(8,128)S(1)}, f32[512,256]{1,0:T(8,128)S(1)}, u32[]{:S(2)}, u32[]{:S(2)}) collective-permute-start(f32[512,256]{1,0:T(8,128)S(1)} %shard_map.107.refs_10_.more_refs_0_), channel_id=1, source_target_pairs={{8,14},{12,15},{24,30},{28,31},{40,46},{44,47},{56,62},{60,63},{72... | collective-permute-start | bytes 1572872 | tf_op jit(solution)/shard_map/ppermute | solution.py:636
  24.7 13.4 %collective-permute-start.7 = (f32[64,128]{1,0:T(8,128)S(1)}, f32[64,128]{1,0:T(8,128)S(1)}, u32[]{:S(2)}, u32[]{:S(2)}) collective-permute-start(f32[64,128]{1,0:T(8,128)S(1)} %copy-done.10), channel_id=1, source_target_pairs={{0,16},{16,32},{32,48},{48,64},{64,80},{80,96},{96,112},{112,0},{1... | collective-permute-start | bytes 98312 | tf_op jit(solution)/shard_map/ppermute | solution.py:572
  24.8 13.3 %copy-start = (f32[8,64,256]{2,1,0:T(8,128)S(1)}, f32[8,64,256]{2,1,0:T(8,128)}, u32[]{:S(2)}) copy-start(f32[8,64,256]{2,1,0:T(8,128)} %east_ref.3) | copy-start | bytes 1572868
  24.8 13.3 %copy-start.1 = (f32[8,64,256]{2,1,0:T(8,128)S(1)}, f32[8,64,256]{2,1,0:T(8,128)}, u32[]{:S(2)}) copy-start(f32[8,64,256]{2,1,0:T(8,128)} %north_ref.3) | copy-start | bytes 1572868
  24.9 13.3 %copy-start.2 = (f32[2,8,64,256]{3,2,1,0:T(8,128)S(1)}, f32[2,8,64,256]{3,2,1,0:T(8,128)}, u32[]{:S(2)}) copy-start(f32[2,8,64,256]{3,2,1,0:T(8,128)} %param.9) | copy-start | bytes 3145732
  24.9 13.3 %copy-start.6 = (f32[7,64,256]{2,1,0:T(8,128)S(1)}, f32[7,64,256]{2,1,0:T(8,128)}, u32[]{:S(2)}) copy-start(f32[7,64,256]{2,1,0:T(8,128)} %mix_ref.3) | copy-start | bytes 1376260
  24.9 13.3 %copy-start.7 = (s32[64,256]{1,0:T(8,128)S(1)}, s32[64,256]{1,0:T(8,128)}, u32[]{:S(2)}) copy-start(s32[64,256]{1,0:T(8,128)} %count_ref.3) | copy-start | bytes 196612
  24.9 13.2 %collective-permute-start.8 = (f32[64,128]{1,0:T(8,128)S(1)}, f32[64,128]{1,0:T(8,128)S(1)}, u32[]{:S(2)}, u32[]{:S(2)}) collective-permute-start(f32[64,128]{1,0:T(8,128)S(1)} %copy-done.9), channel_id=1, source_target_pairs={{16,0},{32,16},{48,32},{64,48},{80,64},{96,80},{112,96},{0,112},{1... | collective-permute-start | bytes 98312 | tf_op jit(solution)/shard_map/ppermute | solution.py:573
  41.9 7.0 %collective-permute-start.9 = (f32[64,128]{1,0:T(8,128)S(1)}, f32[64,128]{1,0:T(8,128)S(1)}, u32[]{:S(2)}, u32[]{:S(2)}) collective-permute-start(f32[64,128]{1,0:T(8,128)S(1)} %get-tuple-element.30), channel_id=1, source_target_pairs={{0,16},{16,32},{32,48},{48,64},{64,80},{80,96},{96,112},{112,0},{1... | collective-permute-start | bytes 98312 | tf_op jit(solution)/shard_map/ppermute | solution.py:572
  41.9 7.0 %collective-permute-start.10 = (f32[64,128]{1,0:T(8,128)S(1)}, f32[64,128]{1,0:T(8,128)S(1)}, u32[]{:S(2)}, u32[]{:S(2)}) collective-permute-start(f32[64,128]{1,0:T(8,128)S(1)} %get-tuple-element.31), channel_id=1, source_target_pairs={{16,0},{32,16},{48,32},{64,48},{80,64},{96,80},{112,96},{0,112},{1... | collective-permute-start | bytes 98312 | tf_op jit(solution)/shard_map/ppermute | solution.py:573
  47.0 1.9 %collective-permute-start.11 = (f32[64,128]{1,0:T(8,128)S(1)}, f32[64,128]{1,0:T(8,128)S(1)}, u32[]{:S(2)}, u32[]{:S(2)}) collective-permute-start(f32[64,128]{1,0:T(8,128)S(1)} %get-tuple-element.32), channel_id=1, source_target_pairs={{0,1},{1,0},{2,3},{3,2},{4,5},{5,4},{6,7},{7,6},{8,9},{9,8},{10,11... | collective-permute-start | bytes 98312 | tf_op jit(solution)/shard_map/ppermute | solution.py:574
  47.0 8.4 %collective-permute-start.12 = (f32[64,128]{1,0:T(8,128)S(1)}, f32[64,128]{1,0:T(8,128)S(1)}, u32[]{:S(2)}, u32[]{:S(2)}) collective-permute-start(f32[64,128]{1,0:T(8,128)S(1)} %get-tuple-element.33), channel_id=1, source_target_pairs={{1,2},{2,1},{3,4},{4,3},{5,6},{6,5},{7,8},{8,7},{9,10},{10,9},{11,... | collective-permute-start | bytes 98312 | tf_op jit(solution)/shard_map/ppermute | solution.py:575
